TPU v7x, 256 devices: a whole 4x4x8 slice. The times are simulated.
256 devices in a mesh: dp: 32 (over z_lo, x, y), tensor: 8 (over z_hi, core).
Axes of the slice: x: 4, y: 4, z: 8 (z_hi: 4, z_lo: 2; z = z_hi * 2 + z_lo), core: 2. Of those that a mesh axis runs over, the one named last changes fastest.
Arguments:
- grad_out: bfloat16 [32768, 6144], P(('dp', 'tensor')), may hold values from -24 to 24
- out_weight: bfloat16 [3072, 6144], P('tensor', 'dp'), may hold values from -0.109375 to 0.109375
- queries: bfloat16 [32768, 3072], P('dp', 'tensor'), may hold values from -21 to 21
- keys_in: bfloat16 [32768, 3072], P('dp', 'tensor'), may hold values from -21 to 21
- values: bfloat16 [32768, 3072], P('dp', 'tensor'), may hold values from -6 to 6
- image_ids: int32 [32768], P('dp'), may hold values from -1 to 2047, as said below
Outputs:
- query_grad: bfloat16 [32768, 3072], P('dp', 'tensor')
- key_grad: bfloat16 [32768, 3072], P('dp', 'tensor')
- value_grad: bfloat16 [32768, 3072], P('dp', 'tensor')
- weight_grad: float32 [3072, 6144], P('tensor', 'dp')
Inputs may be any that keep to these rules, and one draw needn't show every extreme that they name: `image_ids`: images are runs of whole 16-token blocks that never cross a 512-token boundary; an image's number is the index of its first 16-token block in the array, so numbers never fall along the array; any token may be dropped.
All inputs are finite; a program needn't handle non-finite values.
Results may differ from a plain program's by a relative error of at most 0.015.
Values may be sent and summed in bfloat16 or wider, within the bound.
A program may use at most 128 MiB of HBM per device.

v0:
```python
import jax
import jax.numpy as jnp
from jax import lax
from jax.sharding import PartitionSpec as P

HDIM = 128
BUCKET = 512


masked_value = -1e30


def heads_view(matrix):
    bucket_count = matrix.shape[0] // BUCKET
    head_count = matrix.shape[1] // HDIM
    return matrix.reshape(bucket_count, BUCKET, head_count, HDIM).transpose(0, 2, 1, 3)


def rows_view(matrix):
    bucket_count, head_count = (matrix.shape[0], matrix.shape[1])
    return matrix.transpose(0, 2, 1, 3).reshape(bucket_count * BUCKET, head_count * HDIM)


def permitted(first_seg, second_seg, first_pos, second_pos):
    same_image = (first_seg[:, None] == second_seg[None, :]) & (first_seg[:, None] >= 0)
    return same_image | (first_pos[:, None] == second_pos[None, :])


def masked_scores(query_block, key_block, allowed):
    score_scale = HDIM ** (-0.5)
    raw_scores = (
        jnp.einsum("hqd,hkd->hqk", query_block, key_block, preferred_element_type=jnp.float32)
        * score_scale
    )
    return jnp.where(allowed[None], raw_scores, masked_value)


def forward_bucket(query_block, key_block, value_block, segments):
    position = jnp.arange(segments.shape[0])
    scores = masked_scores(
        query_block, key_block, permitted(segments, segments, position, position)
    )
    row_top = jnp.max(scores, axis=-1)
    log_total = row_top + jnp.log(jnp.sum(jnp.exp(scores - row_top[..., None]), axis=-1))
    prob_bf = jnp.exp(scores - log_total[..., None]).astype(jnp.bfloat16)
    out_block = jnp.einsum("hqk,hkd->hqd", prob_bf, value_block, preferred_element_type=jnp.float32)
    return (out_block.astype(jnp.bfloat16), log_total)


def backward_bucket(
    query_block, key_block, value_block, grad_block, out_block, log_total, segments
):
    score_scale = HDIM ** (-0.5)
    position = jnp.arange(segments.shape[0])
    scores = masked_scores(
        query_block, key_block, permitted(segments, segments, position, position)
    )
    probabilities = jnp.exp(scores - log_total[..., None])
    prob_bf = probabilities.astype(jnp.bfloat16)
    row_delta = jnp.sum(grad_block.astype(jnp.float32) * out_block.astype(jnp.float32), axis=-1)
    prob_grad = jnp.einsum(
        "hqd,hkd->hqk", grad_block, value_block, preferred_element_type=jnp.float32
    )
    score_grad = (probabilities * (prob_grad - row_delta[..., None])).astype(jnp.bfloat16)
    query_sum = jnp.einsum(
        "hqk,hkd->hqd", score_grad, key_block, preferred_element_type=jnp.float32
    )
    key_sum = jnp.einsum(
        "hqk,hqd->hkd", score_grad, query_block, preferred_element_type=jnp.float32
    )
    value_sum = jnp.einsum("hqk,hqd->hkd", prob_bf, grad_block, preferred_element_type=jnp.float32)
    return (
        (query_sum * score_scale).astype(jnp.bfloat16),
        (key_sum * score_scale).astype(jnp.bfloat16),
        value_sum.astype(jnp.bfloat16),
    )


def on_device(grad_out, out_weight, queries, keys_in, values, image_ids):
    full_grad = lax.all_gather(grad_out, "tensor", axis=0, tiled=True)
    columns = full_grad
    head_grad = lax.dot_general(
        columns,
        lax.all_gather(out_weight, "dp", axis=1, tiled=True),
        (((1,), (1,)), ((), ())),
        preferred_element_type=jnp.float32,
    ).astype(jnp.bfloat16)
    query_heads = heads_view(queries)
    key_heads = heads_view(keys_in)
    value_heads = heads_view(values)
    grad_heads = heads_view(head_grad)
    segments = image_ids.reshape(-1, BUCKET)
    out_heads, log_total = lax.map(
        lambda bundle: forward_bucket(*bundle), (query_heads, key_heads, value_heads, segments)
    )
    attn_out = rows_view(out_heads)
    bundles = (query_heads, key_heads, value_heads, grad_heads, out_heads, log_total, segments)
    grad_parts = lax.map(lambda bundle: backward_bucket(*bundle), bundles)
    query_grad = rows_view(grad_parts[0])
    key_grad = rows_view(grad_parts[1])
    value_grad = rows_view(grad_parts[2])
    columns = full_grad
    weight_grad = lax.psum_scatter(
        lax.dot_general(
            columns, attn_out, (((0,), (0,)), ((), ())), preferred_element_type=jnp.float32
        ),
        "dp",
        scatter_dimension=0,
        tiled=True,
    ).T
    return (query_grad, key_grad, value_grad, weight_grad)


def solution(mesh):
    placed = (
        P(("dp", "tensor"), None),
        P("tensor", "dp"),
        P("dp", "tensor"),
        P("dp", "tensor"),
        P("dp", "tensor"),
        P("dp"),
    )
    return jax.shard_map(
        on_device,
        mesh=mesh,
        in_specs=placed,
        out_specs=(P("dp", "tensor"), P("dp", "tensor"), P("dp", "tensor"), P("tensor", "dp")),
        check_vma=False,
    )
```

profile of v0, /device:TPU:24, one launch (start us, length us, event | category | flops | bytes accessed | tf_op | source)
XLA Modules:
  0.0 481.1 jit_solution(16842788471271768016)
XLA Ops:
  7.2 0.0 copy-start
  7.2 0.0 all-gather.3.cloned.1.call-start
  7.2 0.7 all-gather.3.cloned.1.call-update
  7.9 0.0 all-gather.5.cloned.1.call-start
  8.0 0.7 all-gather.5.cloned.1.call-update
  8.7 0.0 reduce-scatter.4.cloned.1.call-start
  8.7 1.4 copy.45
  10.1 0.6 reshape.194
  10.7 0.0 copy-start.1
  10.7 1.8 copy.48
  12.5 0.0 copy-done
  12.5 0.3 copy.43
  12.8 0.6 reshape.192
  13.4 0.0 copy-start.4
  13.4 0.7 copy.50
  14.1 0.0 copy-done.1
  14.1 0.3 copy.44
  14.4 0.6 reshape.193
  15.0 0.7 copy.51
  15.7 0.1 broadcast.92.clone.2
  15.8 6.2 %while.26 = (s32[]{:T(128)}, bf16[2,3,512,128]{3,2,1,0:T(8,128)(2,1)S(1)}, f32[2,3,512]{2,1,0:T(4,128)S(1)}, s32[2,512]{1,0:T(2,128)S(1)}, bf16[2,3,512,128]{3,2...) while((s32[]{:T(128)}, ...), condition=%wide.region_3.4_spmd, body=%wide.region_0.3_spmd.sunk | while | flops 412548096 | bytes 15275129 | solution.py:93
  15.9 0.3 fusion.94
  16.2 0.7 fusion.95
  16.9 0.7 exponential_reduce_fusion.2
  17.6 1.3 fusion.96
  19.0 0.3 fusion.94
  19.3 0.7 fusion.95
  20.0 0.7 exponential_reduce_fusion.2
  20.7 1.3 fusion.96
  22.1 0.7 copy.57
  22.7 1.0 copy.77
  23.8 110.1 %all-gather.3.cloned.1.call-done = bf16[1024,6144]{1,0:T(8,128)(2,1)} async-done(((bf16[128,6144]{1,0:T(8,128)(2,1)}), bf16[1024,6144]{1,0:T(8,128)(2,1)}) %all-gather.3.cloned.1.call-update) | async-done | bytes 12582928 | tf_op jit(solution)/shard_map/all_gather | solution.py:80
  133.8 12.2 %convolution_bitcast_fusion = f32[6144,384]{0,1:T(8,128)} fusion(bf16[1024,384]{0,1:T(8,128)(2,1)} %bitcast.160, bf16[1024,6144]{1,0:T(8,128)(2,1)} %all-gather.3.cloned.1.call-done), kind=kOutput, calls=%fused_computation.77 | convolution fusion | flops 4831838208 | bytes 22806528 | tf_op jit(solution)/shard_map/dot_general | solution.py:104
  146.0 9.6 %copy.68 = f32[6144,384]{1,0:T(8,128)} copy(f32[6144,384]{0,1:T(8,128)} %convolution_bitcast_fusion) | data formatting | bytes 18874368
  155.6 0.0 reduce-scatter.4.cloned.1.call-update
  155.7 135.3 %all-gather.5.cloned.1.call-done = bf16[384,6144]{0,1:T(8,128)(2,1)} async-done(((bf16[384,192]{0,1:T(8,128)(2,1)}), bf16[384,6144]{0,1:T(8,128)(2,1)}) %all-gather.5.cloned.1.call-update) | async-done | bytes 4718608 | tf_op jit(solution)/shard_map/all_gather | solution.py:84
  291.0 11.7 %convolution_convert_fusion = bf16[1024,384]{1,0:T(8,128)(2,1)} fusion(bf16[1024,6144]{1,0:T(8,128)(2,1)} %all-gather.3.cloned.1.call-done, bf16[384,6144]{0,1:T(8,128)(2,1)} %all-gather.5.cloned.1.call-done), kind=kOutput, calls=%fused_computation.78 | convolution fusion | flops 4832231424 | bytes 18087936 | tf_op jit(solution)/shard_map/dot_general | solution.py:82
  302.7 1.4 copy.49
  304.1 1.4 reshape.195
  305.6 2.3 copy.52
  307.9 1.0 broadcast.92
  308.9 1.0 broadcast.92.clone
  309.9 1.0 broadcast.92.clone.1
  310.8 14.8 %while.27 = (s32[]{:T(128)}, bf16[2,3,512,128]{3,2,1,0:T(8,128)(2,1)}, bf16[2,3,512,128]{3,2,1,0:T(8,128)(2,1)}, bf16[2,3,512,128]{3,2,1,0:T(8,128)(2,1)}, s32[2...) while((s32[]{:T(128)}, ...), condition=%wide.region_6.7_spmd, body=%wide.region_4.6_spmd.sunk | while | flops 1017314304 | bytes 22864028 | solution.py:98
  310.9 0.3 fusion.109
  311.1 0.6 fusion.107
  311.7 0.3 fusion.108
  312.0 1.3 multiply_convert_fusion.2
  313.3 1.5 fusion.111
  314.8 1.3 fusion.110
  316.2 2.1 fusion.112
  318.3 0.3 fusion.109
  318.6 0.6 fusion.107
  319.1 0.3 fusion.108
  319.5 1.3 multiply_convert_fusion.2
  320.8 1.5 fusion.111
  322.2 1.3 fusion.110
  323.6 2.1 fusion.112
  325.7 1.8 copy.66
  327.5 1.8 copy.67
  329.3 1.8 copy.65
  331.1 1.0 copy.81
  332.1 1.4 copy_bitcast_fusion
  333.5 141.0 %reduce-scatter.4.cloned.1.call-done = f32[192,384]{1,0:T(8,128)} async-done(((f32[6144,384]{1,0:T(8,128)}), f32[192,384]{1,0:T(8,128)}) %reduce-scatter.4.cloned.1.call-update) | async-done | bytes 294928
  (23 shorter events, 0.1 us)
Async XLA Ops:
  7.2 5.4 %copy-start = (bf16[1024,384]{1,0:T(8,128)(2,1)S(1)}, bf16[1024,384]{1,0:T(8,128)(2,1)}, u32[]{:S(2)}) copy-start(bf16[1024,384]{1,0:T(8,128)(2,1)} %param.12) | copy-start | bytes 2359300
  7.2 126.7 %all-gather.3.cloned.1.call-start = ((), (), s32[]{:S(2)}) async-start(), calls=%async_computation.1 | async-start | bytes 14155776 | tf_op jit(solution)/shard_map/all_gather | solution.py:80
  7.9 283.1 %all-gather.5.cloned.1.call-start = ((), (), s32[]{:S(2)}) async-start(), calls=%async_computation.2 | async-start | bytes 4866048 | tf_op jit(solution)/shard_map/all_gather | solution.py:84
  8.7 465.9 %reduce-scatter.4.cloned.1.call-start = ((), (), s32[]{:S(2)}) async-start(), calls=%async_computation.3 | async-start | bytes 9732096
  10.7 3.4 copy-start.1
  13.4 2.3 copy-start.4
  16.1 1.5 copy-start.2
  19.3 1.5 copy-start.2
  310.8 1.2 copy-start.3
  318.3 1.2 copy-start.3
Sparse Core Ops, SparseCore 0:
  9.8 123.9 all-gather.2
  135.6 155.3 all-gather.4
  294.1 180.3 reduce-scatter.3
where the time goes:
time: 490 us; the launch traced here: 481 us
  waiting for transfers between devices  388 us (79%)
  matrix products  41.6 us (8%)
  local copies, waits for them, and re-layouts  34.3 us (7%)
  between operations  13.9 us (3%)
    unnamed x4, waiting for transfers between devices  142 us
    all_gather x1, waiting for transfers between devices, on_device(): lax.all_gather(out_weight, 'dp', axis=1, tiled=True)  135 us
    all_gather x1, waiting for transfers between devices, on_device(): full_grad = lax.all_gather(grad_out, 'tensor', axis=0, tiled=True)  110 us
    unnamed x16, local copies, waits for them, and re-layouts  20.5 us
    dot_general x1, matrix products, on_device(): lax.dot_general(columns, attn_out, (((0,), (0,)), ((), ())), preferred_el...  12.2 us
    dot_general x1, matrix products, on_device(): lax.dot_general(columns, lax.all_gather(out_weight, 'dp', axis=1, tiled=T...  11.7 us
  transfers between devices with their start and end apart: 3, of which 3 were waited for; matrix products, arithmetic and copies ran while one was open for 16% of the time, Pallas kernels for 0%

commit v1 on v0

v1 whole, which is shorter than its diff:
```python
import jax
import jax.numpy as jnp
from jax import lax
from jax.sharding import PartitionSpec as P
import jax.experimental.pallas as pl
import jax.experimental.pallas.tpu as pltpu

HDIM = 128
BUCKET = 512
ROWS = 1024
SUB = 128
WIDTH = 6144
COLS = 384
SHARD = 192
STEPS = 16
AHEAD = 3
MESH = pl.DeviceIdType.MESH
BF = jnp.bfloat16
F32 = jnp.float32
masked_value = -1e30
score_scale = HDIM ** (-0.5)


def dot(a, b, da, db):
    return lax.dot_general(a, b, (((da,), (db,)), ((), ())), preferred_element_type=F32)


def kernel(
    grad_hbm, weight_ref, q_ref, k_ref, v_ref, ids_ref,
    dq_ref, dk_ref, dv_ref, wg_ref,
    grad, weight, attn_t, prob_t, head_grad, stage, parts, pair_out, pair_in,
    local_sem, own_send, own_recv, fwd_send, fwd_recv, sib_send, sib_recv,
    w_send, w_recv, part_send, part_recv, pair_send, pair_recv,
):
    dp = lax.axis_index("dp")
    tensor = lax.axis_index("tensor")
    zl, x, y = dp // 16, (dp // 4) % 4, dp % 4
    zh, core = tensor // 2, tensor % 2
    here = x * 4 + y
    up, down, far = (zh + 1) % 4, (zh + 3) % 4, (zh + 2) % 4
    up_id, down_id = (dp, up * 2 + core), (dp, down * 2 + core)
    sib_id = (dp, zh * 2 + 1 - core)
    pair_id = ((1 - zl) * 16 + here, tensor)

    def plane_id(px, py):
        return (zl * 16 + px * 4 + py, tensor)

    def remote(src, dst, send, recv, device):
        return pltpu.make_async_remote_copy(
            src_ref=src, dst_ref=dst, send_sem=send, recv_sem=recv,
            device_id=device, device_id_type=MESH,
        )

    def place(s):
        group = s // 8
        zc = jnp.where(group == 0, 1 - zl, zl)
        xc = (x + 3 - (s % 8) // 2) % 4
        half = s % 2
        return group, zc, xc, half

    def offset(s):
        _, zc, xc, half = place(s)
        return pl.multiple_of((zc * 4 + xc) * 768 + half * COLS, COLS)

    def block(z, s, first=0, rows=SUB):
        start = pl.multiple_of((z * 2 + core) * SUB + first, rows)
        return grad.at[pl.ds(start, rows), pl.ds(offset(s), COLS)]

    def own_copy(s, way):
        part = block(zh, s)
        return remote(part, part, own_send.at[way, s], own_recv.at[way, s], (up_id, down_id)[way])

    def own_arrival(s, way):
        part = block((down, up)[way], s)
        return remote(part, part, own_send.at[way, s], own_recv.at[way, s], (up_id, down_id)[way])

    def fwd_copy(s, way):
        part = block((down, up)[way], s, way * 64, 64)
        return remote(part, part, fwd_send.at[way, s], fwd_recv.at[way, s], (up_id, down_id)[way])

    def fwd_arrival(s, way):
        part = block(far, s, way * 64, 64)
        return remote(part, part, fwd_send.at[way, s], fwd_recv.at[way, s], (up_id, down_id)[way])

    def sib_copy(s, n):
        part = block((zh, down, up, far)[n], s)
        return remote(part, part, sib_send.at[n, s], sib_recv.at[n, s], sib_id)

    def sib_arrival(s, n):
        z = (zh, down, up, far)[n]
        start = pl.multiple_of((z * 2 + 1 - core) * SUB, SUB)
        part = grad.at[pl.ds(start, SUB), pl.ds(offset(s), COLS)]
        return remote(part, part, sib_send.at[n, s], sib_recv.at[n, s], sib_id)

    def w_slot(slot):
        return weight.at[pl.ds(pl.multiple_of(slot * SHARD, SHARD), SHARD), :]

    def w_copy(group, m):
        slot = jnp.where(group == 0, 1 - zl, zl) * 16 + here
        px, py = (x + 1 + m // 4) % 4, (y + m) % 4
        return remote(
            w_slot(slot), w_slot(slot), w_send.at[group, m], w_recv.at[slot], plane_id(px, py)
        )

    def pair_w():
        slot = dp
        return remote(w_slot(slot), w_slot(slot), w_send.at[1, 12], w_recv.at[slot], pair_id)

    def w_arrival(slot):
        return remote(w_slot(slot), w_slot(slot), w_send.at[0, 0], w_recv.at[slot], pair_id)

    def part_copy(s, n):
        group, zc, xc, half = place(s)
        return remote(
            stage.at[s, pl.ds(n * SHARD, SHARD), :], parts.at[group, here],
            part_send.at[s, n], part_recv.at[group, here], plane_id(xc, half * 2 + n),
        )

    def part_arrival(group, source):
        return remote(
            parts.at[group, source], parts.at[group, source],
            part_send.at[0, 0], part_recv.at[group, source], pair_id,
        )

    def pair_copy():
        return remote(pair_out, pair_in, pair_send, pair_recv, pair_id)

    load = pltpu.make_async_copy(
        grad_hbm, grad.at[pl.ds(pl.multiple_of(tensor * SUB, SUB), SUB), :], local_sem
    )
    load.start()

    barrier = pltpu.get_barrier_semaphore()
    for device in (up_id, down_id, sib_id, pair_id):
        pl.semaphore_signal(barrier, inc=1, device_id=device, device_id_type=MESH)
    for m in range(16):
        if m != 12:
            pl.semaphore_signal(
                barrier, inc=1, device_id=plane_id((x + 1 + m // 4) % 4, (y + m) % 4),
                device_id_type=MESH,
            )
    weight[pl.ds(pl.multiple_of(dp * SHARD, SHARD), SHARD), :] = weight_ref[...]
    load.wait()
    pl.semaphore_wait(barrier, 19)

    @pl.loop(0, AHEAD)
    def _(s):
        own_copy(s, 0).start()
        own_copy(s, 1).start()

    pair_w().start()

    @pl.loop(0, 16)
    def _(m):
        @pl.when(m != 12)
        def _():
            w_copy(1, m).start()

    @pl.loop(0, STEPS)
    def _(s):
        sib_copy(s, 0).start()

    w_arrival((1 - zl) * 16 + here).wait_recv()

    @pl.loop(0, 16)
    def _(m):
        @pl.when(m != 12)
        def _():
            w_copy(0, m).start()

    def head_slices(i):
        bucket, head = i // 3, i % 3
        rows = pl.ds(pl.multiple_of(bucket * BUCKET, BUCKET), BUCKET)
        cols = pl.ds(pl.multiple_of(head * HDIM, HDIM), HDIM)
        return bucket, rows, cols

    @pl.loop(0, 6)
    def _(i):
        bucket, rows, cols = head_slices(i)
        ids = ids_ref[bucket]
        position = lax.broadcasted_iota(jnp.int32, (1, BUCKET), 1)
        label = jnp.where(ids < 0, -1 - position, ids).astype(F32)
        column = jnp.broadcast_to(label, (HDIM, BUCKET)).T
        column = jnp.concatenate([column] * (BUCKET // HDIM), axis=1)
        scores = dot(k_ref[rows, cols], q_ref[rows, cols], 1, 1) * score_scale
        scores = jnp.where(column == label, scores, masked_value)
        weights = jnp.exp(scores - jnp.max(scores, axis=0, keepdims=True))
        prob = weights / jnp.sum(weights, axis=0, keepdims=True)
        prob_t[i] = prob
        attn_t[cols, rows] = dot(v_ref[rows, cols], prob.astype(BF), 0, 0).astype(BF)

    head_grad[...] = jnp.zeros_like(head_grad)

    def matmuls(s):
        at = offset(s)
        group, zc, xc, half = place(s)
        w_part = weight[pl.ds(at, COLS), :]
        for t in range(4):
            rows = pl.ds(t * 256, 256)
            head_grad[rows, :] += dot(grad[rows, pl.ds(at, COLS)], w_part, 1, 0)
        for h in range(3):
            part = dot(attn_t[h * HDIM:(h + 1) * HDIM, :], grad[:, pl.ds(at, COLS)], 1, 0)
            stage[s, :, h * HDIM:(h + 1) * HDIM] = part.T.astype(BF)
        for n in range(2):
            mine = (xc == x) & (half * 2 + n == y)

            @pl.when(mine)
            def _():
                parts[group, here] = stage[s, n * SHARD:(n + 1) * SHARD, :]

            @pl.when(jnp.logical_not(mine))
            def _():
                part_copy(s, n).start()

    def collect(group):
        @pl.loop(0, 16)
        def _(source):
            @pl.when(source != here)
            def _():
                part_arrival(group, source).wait_recv()

    def part_sum(group, rows):
        def add(source, total):
            return total + parts[group, source, rows, :].astype(F32)

        return lax.fori_loop(0, 16, add, jnp.zeros((48, COLS), F32))

    @pl.loop(0, STEPS + 1)
    def _(s):
        @pl.when(s < STEPS)
        def _():
            own_arrival(s, 0).wait_recv()
            own_arrival(s, 1).wait_recv()
            fwd_copy(s, 0).start()
            fwd_copy(s, 1).start()
            sib_copy(s, 1).start()
            sib_copy(s, 2).start()

        @pl.when(s + AHEAD < STEPS)
        def _():
            own_copy(s + AHEAD, 0).start()
            own_copy(s + AHEAD, 1).start()

        @pl.when(s >= 1)
        def _():
            t = s - 1
            fwd_arrival(t, 0).wait_recv()
            fwd_arrival(t, 1).wait_recv()
            sib_copy(t, 3).start()
            group, zc, xc, half = place(t)
            for n in range(2):
                yc = half * 2 + n

                @pl.when((xc != x) | (yc != y))
                def _():
                    w_arrival(zc * 16 + xc * 4 + yc).wait_recv()

            for n in range(4):
                sib_arrival(t, n).wait_recv()
            matmuls(t)

        @pl.when(s == 12)
        def _():
            collect(0)

            @pl.loop(0, 4)
            def _(r):
                rows = pl.ds(pl.multiple_of(r * 48, 48), 48)
                pair_out[rows, :] = part_sum(0, rows).astype(BF)

            pair_copy().start()

    @pl.loop(0, 6)
    def _(i):
        bucket, rows, cols = head_slices(i)
        grad_h = head_grad[rows, cols].astype(BF)
        prob = prob_t[i]
        prob_grad = dot(v_ref[rows, cols], grad_h, 1, 1)
        delta = jnp.sum(
            grad_h.astype(F32).T * attn_t[cols, rows].astype(F32), axis=0, keepdims=True
        )
        score_grad = (prob * (prob_grad - delta)).astype(BF)
        dv_ref[rows, cols] = dot(prob.astype(BF), grad_h, 1, 0).astype(BF)
        dk_ref[rows, cols] = (dot(score_grad, q_ref[rows, cols], 1, 0) * score_scale).astype(BF)
        dq = dot(k_ref[rows, cols], score_grad, 0, 0) * score_scale
        dq_ref[rows, cols] = dq.T.astype(BF)

    collect(1)
    pair_copy().wait_recv()

    @pl.loop(0, 4)
    def _(r):
        rows = pl.ds(pl.multiple_of(r * 48, 48), 48)
        wg_ref[rows, :] = part_sum(1, rows) + pair_in[rows, :].astype(F32)

    pair_copy().wait_send()
    pair_w().wait_send()

    @pl.loop(0, 16)
    def _(m):
        @pl.when(m != 12)
        def _():
            w_copy(0, m).wait_send()
            w_copy(1, m).wait_send()

    @pl.loop(0, STEPS)
    def _(s):
        for way in range(2):
            own_copy(s, way).wait_send()
            fwd_copy(s, way).wait_send()
        for n in range(4):
            sib_copy(s, n).wait_send()
        group, zc, xc, half = place(s)
        for n in range(2):
            @pl.when((xc != x) | (half * 2 + n != y))
            def _():
                part_copy(s, n).wait_send()


def on_device(grad_out, out_weight, queries, keys_in, values, image_ids):
    vmem = pl.BlockSpec(memory_space=pltpu.VMEM)
    dma = pltpu.SemaphoreType.DMA
    outs = pl.pallas_call(
        kernel,
        out_shape=(
            jax.ShapeDtypeStruct((ROWS, COLS), BF),
            jax.ShapeDtypeStruct((ROWS, COLS), BF),
            jax.ShapeDtypeStruct((ROWS, COLS), BF),
            jax.ShapeDtypeStruct((SHARD, COLS), F32),
        ),
        in_specs=[pl.BlockSpec(memory_space=pl.ANY)] + [vmem] * 5,
        out_specs=(vmem,) * 4,
        scratch_shapes=[
            pltpu.VMEM((ROWS, WIDTH), BF),
            pltpu.VMEM((WIDTH, COLS), BF),
            pltpu.VMEM((COLS, ROWS), BF),
            pltpu.VMEM((6, BUCKET, BUCKET), F32),
            pltpu.VMEM((ROWS, COLS), F32),
            pltpu.VMEM((STEPS, COLS, COLS), BF),
            pltpu.VMEM((2, 16, SHARD, COLS), BF),
            pltpu.VMEM((SHARD, COLS), BF),
            pltpu.VMEM((SHARD, COLS), BF),
            dma,
            dma((2, STEPS)), dma((2, STEPS)),
            dma((2, STEPS)), dma((2, STEPS)),
            dma((4, STEPS)), dma((4, STEPS)),
            dma((2, 16)), dma((32,)),
            dma((STEPS, 2)), dma((2, 16)),
            dma, dma,
        ],
        compiler_params=pltpu.CompilerParams(
            collective_id=0, has_side_effects=True, vmem_limit_bytes=60 * 2**20
        ),
        cost_estimate=pl.CostEstimate(
            flops=13 * 10**9, bytes_accessed=30 * 10**6, transcendentals=1572864
        ),
        name="attention_backward",
    )(
        grad_out, out_weight.T, queries, keys_in, values,
        image_ids.reshape(2, 1, BUCKET),
    )
    return (outs[0], outs[1], outs[2], outs[3].T)


def solution(mesh):
    placed = (
        P(("dp", "tensor"), None),
        P("tensor", "dp"),
        P("dp", "tensor"),
        P("dp", "tensor"),
        P("dp", "tensor"),
        P("dp"),
    )
    return jax.shard_map(
        on_device,
        mesh=mesh,
        in_specs=placed,
        out_specs=(P("dp", "tensor"), P("dp", "tensor"), P("dp", "tensor"), P("tensor", "dp")),
        check_vma=False,
    )
```

time: 490 us -> 175 us (0.36)
  the two profiles are of different devices: /device:TPU:24 before, /device:TPU:51 now
where the time goes in v1:
time: 175 us
  Pallas kernels  169 us (97%)
  local copies, waits for them, and re-layouts  4.69 us (3%)
    pallas_call x1, Pallas kernels, on_device(): pl.pallas_call(kernel, out_shape=(jax.ShapeDtypeStruct((ROWS, COLS), BF),...  169 us
    unnamed x10, local copies, waits for them, and re-layouts  4.69 us

profile of v1, /device:TPU:51, one launch (start us, length us, event | category | flops | bytes accessed | tf_op | source)
XLA Modules:
  0.0 174.8 jit_solution(2621557348951265836)
XLA Ops:
  0.6 169.4 %attention_backward.1 = (bf16[1024,384]{1,0:T(8,128)(2,1)}, bf16[1024,384]{1,0:T(8,128)(2,1)}, bf16[1024,384]{1,0:T(8,128)(2,1)}, f32[192,384]{1,0:T(8,128)}) custom-call(bf16[128,6144]{1,0:T(8,128)(2,1)} %grad_hbm.1, bf16[192,384]{1,0:T(8,128)(2,1)} %bitcast.4, bf16[1024,384]{1,0:T(8,128)(2,1)} %q_ref.1, bf16[1024,384]{1,0:T(8,128)(2,1)} %k_ref.1, ...), custom_call_target="tpu_custom_call" | custom-call | flops 12999999488 | bytes 30000000 | tf_op jit(solution)/shard_map/attention_backward/pallas_call | solution.py:323
  170.1 0.0 copy-start.1
  170.1 0.0 copy-start
  170.1 2.2 %copy.14 = bf16[1024,384]{1,0:T(8,128)(2,1)} copy(bf16[1024,384]{1,0:T(8,128)(2,1)} %get-tuple-element.16) | data formatting | bytes 1572864
  172.3 0.0 copy-done.1
  172.3 0.0 copy-start.2
  172.3 0.9 copy.15
  173.2 0.0 copy-done
  173.2 0.9 copy.16
  174.1 0.0 copy-done.2
  174.1 0.7 copy.17
Async XLA Ops:
  170.1 2.2 %copy-start.1 = (bf16[1024,384]{1,0:T(8,128)(2,1)S(1)}, bf16[1024,384]{1,0:T(8,128)(2,1)}, u32[]{:S(2)}) copy-start(bf16[1024,384]{1,0:T(8,128)(2,1)} %get-tuple-element.17) | copy-start | bytes 2359300
  170.1 3.1 %copy-start = (bf16[1024,384]{1,0:T(8,128)(2,1)S(1)}, bf16[1024,384]{1,0:T(8,128)(2,1)}, u32[]{:S(2)}) copy-start(bf16[1024,384]{1,0:T(8,128)(2,1)} %get-tuple-element.18) | copy-start | bytes 2359300
  172.3 1.8 %copy-start.2 = (f32[192,384]{1,0:T(8,128)S(1)}, f32[192,384]{1,0:T(8,128)}, u32[]{:S(2)}) copy-start(f32[192,384]{1,0:T(8,128)} %get-tuple-element.11) | copy-start | bytes 884740

commit v2 on v1

v2 whole, which is shorter than its diff:
```python
import jax
import jax.numpy as jnp
from jax import lax
from jax.sharding import PartitionSpec as P
import jax.experimental.pallas as pl
import jax.experimental.pallas.tpu as pltpu

HDIM = 128
BUCKET = 512
ROWS = 1024
SUB = 128
WIDTH = 6144
COLS = 384
SHARD = 192
STEPS = 16
AHEAD = 3
MESH = pl.DeviceIdType.MESH
BF = jnp.bfloat16
F32 = jnp.float32
masked_value = -1e30
score_scale = HDIM ** (-0.5)


def dot(a, b, da, db):
    return lax.dot_general(a, b, (((da,), (db,)), ((), ())), preferred_element_type=F32)


def kernel(
    grad_hbm, q_hbm, k_hbm, v_hbm, weight_ref, ids_ref,
    dq_hbm, dk_hbm, dv_hbm, wg_ref,
    grad, weight, attn_t, prob_t, head_grad, stage, parts, pair_out, pair_in, early_sum,
    q_ref, k_ref, v_ref, dq_ref, dk_ref, dv_ref, local_sem, in_sem, out_sem, hop_send, hop_recv, sib_send, sib_recv,
    w_send, w_recv, part_send, part_recv, pair_send, pair_recv,
):
    dp = lax.axis_index("dp")
    tensor = lax.axis_index("tensor")
    zl, x, y = dp // 16, (dp // 4) % 4, dp % 4
    zh, core = tensor // 2, tensor % 2
    here = x * 4 + y
    u, v = jnp.where(core == 0, x, y), jnp.where(core == 0, y, x)
    up, down, far = (zh + 1) % 4, (zh + 3) % 4, (zh + 2) % 4
    ahead, back = jnp.where(core == 0, up, down), jnp.where(core == 0, down, up)
    next_id = (dp, ahead * 2 + core)
    up_id, down_id = (dp, up * 2 + core), (dp, down * 2 + core)
    sib_id = (dp, zh * 2 + 1 - core)
    pair_id = ((1 - zl) * 16 + here, tensor)

    def plane_id(px, py):
        return (zl * 16 + px * 4 + py, tensor)

    def remote(src, dst, send, recv, device):
        return pltpu.make_async_remote_copy(
            src_ref=src, dst_ref=dst, send_sem=send, recv_sem=recv,
            device_id=device, device_id_type=MESH,
        )

    def place(s):
        group = s // 8
        zc = jnp.where(group == 0, 1 - zl, zl)
        xc = (x + 3 - (s % 8) // 2) % 4
        half = (s + 1 + y // 2) % 2
        return group, zc, xc, half

    def chunk(s):
        _, zc, xc, half = place(s)
        return (zc * 4 + xc) * 2 + half

    def block(z, s, first=0, rows=SUB):
        start = pl.multiple_of((z * 2 + core) * SUB + first, rows)
        return grad.at[chunk(s), pl.ds(start, rows), :]

    def hop_copy(s, n):
        part = block((zh, back, far)[n], s)
        return remote(part, part, hop_send.at[n, s], hop_recv.at[n, s], next_id)

    def hop_arrival(s, n):
        part = block((back, far, ahead)[n], s)
        return remote(part, part, hop_send.at[n, s], hop_recv.at[n, s], next_id)

    def sib_copy(s, n):
        part = block((zh, back, far, ahead)[n], s)
        return remote(part, part, sib_send.at[n, s], sib_recv.at[n, s], sib_id)

    def sib_arrival(s, n):
        z = (zh, back, far, ahead)[n]
        start = pl.multiple_of((z * 2 + 1 - core) * SUB, SUB)
        part = grad.at[chunk(s), pl.ds(start, SUB), :]
        return remote(part, part, sib_send.at[n, s], sib_recv.at[n, s], sib_id)

    def w_slot(slot):
        return weight.at[pl.ds(pl.multiple_of(slot * SHARD, SHARD), SHARD), :]

    def spot(u_at, v_at):
        return jnp.where(core == 0, u_at * 4 + v_at, v_at * 4 + u_at)

    def w_copy(group, m):
        zc = jnp.where(group == 0, 1 - zl, zl)
        first = m // 4 == 0
        slot = w_slot(zc * 16 + spot(u, jnp.where(first, v, (v + m) % 4)))
        to = spot((u + m // 4) % 4, jnp.where(first, (v + m) % 4, v))
        return remote(
            slot, slot, w_send.at[group, m],
            w_recv.at[zc * 16 + spot(u, jnp.where(first, v, (v + m) % 4))], (zl * 16 + to, tensor),
        )

    def w_first(group):
        for m in range(1, 4):
            w_copy(group, m).start()

    def w_second(group):
        zc = jnp.where(group == 0, 1 - zl, zl)
        for m in range(1, 4):
            w_arrival(zc * 16 + spot(u, (v + m) % 4)).wait_recv()

        @pl.loop(4, 16)
        def _(m):
            w_copy(group, m).start()

    def pair_w():
        slot = dp
        return remote(w_slot(slot), w_slot(slot), w_send.at[1, 0], w_recv.at[slot], pair_id)

    def w_arrival(slot):
        return remote(w_slot(slot), w_slot(slot), w_send.at[0, 0], w_recv.at[slot], pair_id)

    def part_copy(s, n):
        group, zc, xc, half = place(s)
        return remote(
            stage.at[s, pl.ds(n * SHARD, SHARD), :], parts.at[group, here],
            part_send.at[s, n], part_recv.at[group, here], plane_id(xc, half * 2 + n),
        )

    def part_arrival(group, source):
        return remote(
            parts.at[group, source], parts.at[group, source],
            part_send.at[0, 0], part_recv.at[group, source], pair_id,
        )

    def pair_copy():
        return remote(pair_out, pair_in, pair_send, pair_recv, pair_id)

    def load(s):
        return pltpu.make_async_copy(
            grad_hbm.at[:, pl.ds(pl.multiple_of(chunk(s) * COLS, COLS), COLS)],
            block(zh, s), local_sem.at[s],
        )

    @pl.loop(0, STEPS)
    def _(s):
        load(s).start()

    heads_in = [
        pltpu.make_async_copy(src, dst, in_sem.at[n])
        for n, (src, dst) in enumerate(((q_hbm, q_ref), (k_hbm, k_ref), (v_hbm, v_ref)))
    ]
    heads_out = [
        pltpu.make_async_copy(src, dst, out_sem.at[n])
        for n, (src, dst) in enumerate(((dq_ref, dq_hbm), (dk_ref, dk_hbm), (dv_ref, dv_hbm)))
    ]
    barrier = pltpu.get_barrier_semaphore()
    for device in (up_id, down_id, sib_id, pair_id):
        pl.semaphore_signal(barrier, inc=1, device_id=device, device_id_type=MESH)
    for m in range(16):
        if m != 12:
            pl.semaphore_signal(
                barrier, inc=1, device_id=plane_id((x + 1 + m // 4) % 4, (y + m) % 4),
                device_id_type=MESH,
            )
    for copy in heads_in:
        copy.start()
    weight[pl.ds(pl.multiple_of(dp * SHARD, SHARD), SHARD), :] = weight_ref[...]
    @pl.loop(0, STEPS)
    def _(s):
        load(s).wait()

    pl.semaphore_wait(barrier, 19)

    @pl.loop(0, AHEAD)
    def _(s):
        hop_copy(s, 0).start()

    pair_w().start()

    w_first(1)

    @pl.loop(0, STEPS)
    def _(s):
        sib_copy(s, 0).start()

    w_arrival((1 - zl) * 16 + here).wait_recv()
    w_first(0)

    def head_slices(i):
        bucket, head = i // 3, i % 3
        rows = pl.ds(pl.multiple_of(bucket * BUCKET, BUCKET), BUCKET)
        cols = pl.ds(pl.multiple_of(head * HDIM, HDIM), HDIM)
        return bucket, rows, cols

    for copy in heads_in:
        copy.wait()

    @pl.loop(0, 6)
    def _(i):
        bucket, rows, cols = head_slices(i)
        ids = ids_ref[bucket]
        position = lax.broadcasted_iota(jnp.int32, (1, BUCKET), 1)
        label = jnp.where(ids < 0, -1 - position, ids).astype(F32)
        column = jnp.broadcast_to(label, (HDIM, BUCKET)).T
        column = jnp.concatenate([column] * (BUCKET // HDIM), axis=1)
        scores = dot(k_ref[rows, cols], q_ref[rows, cols], 1, 1) * score_scale
        scores = jnp.where(column == label, scores, masked_value)
        weights = jnp.exp(scores - jnp.max(scores, axis=0, keepdims=True))
        prob = weights / jnp.sum(weights, axis=0, keepdims=True)
        prob_t[i] = prob
        attn_t[cols, rows] = dot(v_ref[rows, cols], prob.astype(BF), 0, 0).astype(BF)

    head_grad[...] = jnp.zeros_like(head_grad)

    def weight_part(s):
        at = chunk(s)
        group, zc, xc, half = place(s)
        for h in range(3):
            part = dot(attn_t[h * HDIM:(h + 1) * HDIM, :], grad[at], 1, 0)
            stage[s, :, h * HDIM:(h + 1) * HDIM] = part.T.astype(BF)
        for n in range(2):
            mine = (xc == x) & (half * 2 + n == y)

            @pl.when(mine)
            def _():
                parts[group, here] = stage[s, n * SHARD:(n + 1) * SHARD, :]

            @pl.when(jnp.logical_not(mine))
            def _():
                part_copy(s, n).start()

    def head_part(s):
        at = chunk(s)
        group, zc, xc, half = place(s)
        for n in range(2):
            yc = half * 2 + n

            @pl.when(jnp.where(core == 0, xc, yc) != u)
            def _():
                w_arrival(zc * 16 + xc * 4 + yc).wait_recv()

        w_part = weight[pl.ds(pl.multiple_of(at * COLS, COLS), COLS), :]
        for t in range(4):
            rows = pl.ds(t * 256, 256)
            head_grad[rows, :] += dot(grad[at, rows, :], w_part, 1, 0)

    def source_at(i):
        return ((x + 1 + i // 4) % 4) * 4 + i % 4

    def collect(group, first, last):
        @pl.loop(first, last)
        def _(i):
            @pl.when(source_at(i) != here)
            def _():
                part_arrival(group, source_at(i)).wait_recv()

    def part_sum(group, rows, first, last):
        def add(i, total):
            return total + parts[group, source_at(i), rows, :].astype(F32)

        return lax.fori_loop(first, last, add, jnp.zeros((48, COLS), F32))

    def sent(s):
        for n in range(3):
            hop_copy(s, n).wait_send()
        for n in range(4):
            sib_copy(s, n).wait_send()
        group, zc, xc, half = place(s)
        for n in range(2):
            @pl.when((xc != x) | (half * 2 + n != y))
            def _():
                part_copy(s, n).wait_send()

    @pl.loop(0, STEPS + 2)
    def _(s):
        @pl.when(s < STEPS)
        def _():
            hop_arrival(s, 0).wait_recv()
            hop_copy(s, 1).start()
            sib_copy(s, 1).start()

        @pl.when((s >= 1) & (s <= STEPS))
        def _():
            hop_arrival(s - 1, 1).wait_recv()
            hop_copy(s - 1, 2).start()
            sib_copy(s - 1, 2).start()

        @pl.when(s == 1)
        def _():
            w_second(0)

        @pl.when(s == 2)
        def _():
            w_second(1)

        @pl.when(s + AHEAD < STEPS)
        def _():
            hop_copy(s + AHEAD, 0).start()

        @pl.when(s >= 2)
        def _():
            t = s - 2
            hop_arrival(t, 2).wait_recv()
            sib_copy(t, 3).start()
            for n in range(4):
                sib_arrival(t, n).wait_recv()
            weight_part(t)

        @pl.when(s > 9)
        def _():
            @pl.loop(jnp.where(s == STEPS + 1, 15, 2 * s - 20), jnp.where(s == STEPS, 15, 2 * s - 18))
            def _(r):
                head_part(r)

        @pl.when(s == 13)
        def _():
            pair_w().wait_send()

            @pl.loop(1, 16)
            def _(m):
                w_copy(0, m).wait_send()
                w_copy(1, m).wait_send()

        @pl.when(s == 14)
        def _():
            collect(0, 0, 16)

            @pl.loop(0, 4)
            def _(r):
                rows = pl.ds(pl.multiple_of(r * 48, 48), 48)
                pair_out[rows, :] = part_sum(0, rows, 0, 16).astype(BF)

            pair_copy().start()

        @pl.when(s == STEPS)
        def _():
            collect(1, 0, 12)

            @pl.loop(0, 4)
            def _(r):
                rows = pl.ds(pl.multiple_of(r * 48, 48), 48)
                early_sum[rows, :] = part_sum(1, rows, 0, 12)

    @pl.loop(0, 6, unroll=2)
    def _(i):
        bucket, rows, cols = head_slices(i)
        grad_h = head_grad[rows, cols].astype(BF)
        prob = prob_t[i]
        prob_grad = dot(v_ref[rows, cols], grad_h, 1, 1)
        delta = jnp.sum(
            grad_h.astype(F32).T * attn_t[cols, rows].astype(F32), axis=0, keepdims=True
        )
        score_grad = (prob * (prob_grad - delta)).astype(BF)
        dv_ref[rows, cols] = dot(prob.astype(BF), grad_h, 1, 0).astype(BF)
        dk_ref[rows, cols] = (dot(score_grad, q_ref[rows, cols], 1, 0) * score_scale).astype(BF)
        dq = dot(k_ref[rows, cols], score_grad, 0, 0) * score_scale
        dq_ref[rows, cols] = dq.T.astype(BF)

    for copy in heads_out:
        copy.start()
    collect(1, 12, 16)
    pair_copy().wait_recv()

    @pl.loop(0, 4)
    def _(r):
        rows = pl.ds(pl.multiple_of(r * 48, 48), 48)
        late = part_sum(1, rows, 12, 16) + pair_in[rows, :].astype(F32)
        wg_ref[rows, :] = early_sum[rows, :] + late

    for copy in heads_out:
        copy.wait()
    pair_copy().wait_send()

    @pl.loop(0, STEPS)
    def _(s):
        sent(s)


def place_outputs(*refs):
    ins, outs, held, sems = refs[:4], refs[4:8], refs[8:12], refs[12]
    loads = [pltpu.make_async_copy(ins[n], held[n], sems.at[0, n]) for n in range(4)]
    stores = [pltpu.make_async_copy(held[n], outs[n], sems.at[1, n]) for n in range(4)]
    for copy in loads:
        copy.start()
    for n in range(4):
        loads[n].wait()
        stores[n].start()
    for copy in stores:
        copy.wait()


def on_device(grad_out, out_weight, queries, keys_in, values, image_ids):
    vmem = pl.BlockSpec(memory_space=pltpu.VMEM)
    hbm = pl.BlockSpec(memory_space=pl.ANY)
    dma = pltpu.SemaphoreType.DMA
    outs = pl.pallas_call(
        kernel,
        out_shape=(
            jax.ShapeDtypeStruct((ROWS, COLS), BF),
            jax.ShapeDtypeStruct((ROWS, COLS), BF),
            jax.ShapeDtypeStruct((ROWS, COLS), BF),
            jax.ShapeDtypeStruct((SHARD, COLS), F32),
        ),
        in_specs=[hbm] * 4 + [vmem] * 2,
        out_specs=(hbm,) * 3 + (vmem,),
        scratch_shapes=[
            pltpu.VMEM((STEPS, ROWS, COLS), BF),
            pltpu.VMEM((WIDTH, COLS), BF),
            pltpu.VMEM((COLS, ROWS), BF),
            pltpu.VMEM((6, BUCKET, BUCKET), F32),
            pltpu.VMEM((ROWS, COLS), F32),
            pltpu.VMEM((STEPS, COLS, COLS), BF),
            pltpu.VMEM((2, 16, SHARD, COLS), BF),
            pltpu.VMEM((SHARD, COLS), BF),
            pltpu.VMEM((SHARD, COLS), BF),
            pltpu.VMEM((SHARD, COLS), F32),
        ] + [pltpu.VMEM((ROWS, COLS), BF)] * 6 + [
            dma((STEPS,)), dma((3,)), dma((3,)),
            dma((3, STEPS)), dma((3, STEPS)),
            dma((4, STEPS)), dma((4, STEPS)),
            dma((2, 16)), dma((32,)),
            dma((STEPS, 2)), dma((2, 16)),
            dma, dma,
        ],
        compiler_params=pltpu.CompilerParams(
            collective_id=0, has_side_effects=True, vmem_limit_bytes=60 * 2**20
        ),
        cost_estimate=pl.CostEstimate(
            flops=13 * 10**9, bytes_accessed=30 * 10**6, transcendentals=1572864
        ),
        name="attention_backward",
    )(
        grad_out, queries, keys_in, values, out_weight.T,
        image_ids.reshape(2, 1, BUCKET),
    )
    outs = pl.pallas_call(
        place_outputs,
        out_shape=tuple(jax.ShapeDtypeStruct(out.shape, out.dtype) for out in outs),
        in_specs=[hbm] * 4,
        out_specs=(hbm,) * 4,
        scratch_shapes=[pltpu.VMEM(out.shape, out.dtype) for out in outs] + [dma((2, 4))],
        name="place_outputs",
    )(*outs)
    return (outs[0], outs[1], outs[2], outs[3].T)


def solution(mesh):
    placed = (
        P(("dp", "tensor"), None),
        P("tensor", "dp"),
        P("dp", "tensor"),
        P("dp", "tensor"),
        P("dp", "tensor"),
        P("dp"),
    )
    return jax.shard_map(
        on_device,
        mesh=mesh,
        in_specs=placed,
        out_specs=(P("dp", "tensor"), P("dp", "tensor"), P("dp", "tensor"), P("tensor", "dp")),
        check_vma=False,
    )
```

time: 175 us -> 156 us (0.89)
  the two profiles are of different devices: /device:TPU:51 before, /device:TPU:29 now
where the time goes in v2:
time: 156 us
  Pallas kernels  156 us (100%)
    pallas_call x1, Pallas kernels, on_device(): pl.pallas_call(kernel, out_shape=(jax.ShapeDtypeStruct((ROWS, COLS), BF),...  153 us

profile of v2, /device:TPU:29, one launch (start us, length us, event | category | flops | bytes accessed | tf_op | source)
XLA Modules:
  0.0 156.3 jit_solution(12438785941761311611)
XLA Ops:
  0.6 152.9 %attention_backward.1 = (bf16[1024,384]{1,0:T(8,128)(2,1)}, bf16[1024,384]{1,0:T(8,128)(2,1)}, bf16[1024,384]{1,0:T(8,128)(2,1)}, f32[192,384]{1,0:T(8,128)}) custom-call(bf16[128,6144]{1,0:T(8,128)(2,1)} %grad_hbm.1, bf16[1024,384]{1,0:T(8,128)(2,1)} %q_hbm.1, bf16[1024,384]{1,0:T(8,128)(2,1)} %k_hbm.1, bf16[1024,384]{1,0:T(8,128)(2,1)} %v_hbm.1, ...), custom_call_target="tpu_custom_call" | custom-call | flops 12999999488 | bytes 30000000 | tf_op jit(solution)/shard_map/attention_backward/pallas_call | solution.py:400
  153.6 2.7 %place_outputs.1 = (bf16[1024,384]{1,0:T(8,128)(2,1)}, bf16[1024,384]{1,0:T(8,128)(2,1)}, bf16[1024,384]{1,0:T(8,128)(2,1)}, f32[192,384]{1,0:T(8,128)}) custom-call(bf16[1024,384]{1,0:T(8,128)(2,1)} %get-tuple-element.12.refs_0_, bf16[1024,384]{1,0:T(8,128)(2,1)} %get-tuple-element.13.refs_1_, bf16[1024,384]{1,0:T(8,128)(2,1)} %get-tuple-element.14.refs_2_, ...), custom_call_target="tpu_custom_call" | custom-call | tf_op jit(solution)/shard_map/place_outputs/pallas_call | solution.py:440

commit v3 on v2

--- a/solution.py
+++ b/solution.py
@@ -13,7 +13,7 @@
 COLS = 384
 SHARD = 192
 STEPS = 16
-AHEAD = 3
+AHEAD = 5
 MESH = pl.DeviceIdType.MESH
 BF = jnp.bfloat16
 F32 = jnp.float32
@@ -175,20 +175,13 @@
 
     pl.semaphore_wait(barrier, 19)
 
-    @pl.loop(0, AHEAD)
+    hop_copy(0, 0).start()
+    pair_w().start()
+    w_first(1)
+
+    @pl.loop(1, AHEAD)
     def _(s):
         hop_copy(s, 0).start()
-
-    pair_w().start()
-
-    w_first(1)
-
-    @pl.loop(0, STEPS)
-    def _(s):
-        sib_copy(s, 0).start()
-
-    w_arrival((1 - zl) * 16 + here).wait_recv()
-    w_first(0)
 
     def head_slices(i):
         bucket, head = i // 3, i % 3
@@ -275,12 +268,13 @@
             def _():
                 part_copy(s, n).wait_send()
 
-    @pl.loop(0, STEPS + 2)
+    @pl.loop(0, STEPS + 3)
     def _(s):
         @pl.when(s < STEPS)
         def _():
             hop_arrival(s, 0).wait_recv()
             hop_copy(s, 1).start()
+            sib_copy(s, 0).start()
             sib_copy(s, 1).start()
 
         @pl.when((s >= 1) & (s <= STEPS))
@@ -291,9 +285,14 @@
 
         @pl.when(s == 1)
         def _():
+            w_arrival((1 - zl) * 16 + here).wait_recv()
+            w_first(0)
+
+        @pl.when(s == 3)
+        def _():
             w_second(0)
 
-        @pl.when(s == 2)
+        @pl.when(s == 5)
         def _():
             w_second(1)
 
@@ -301,18 +300,23 @@
         def _():
             hop_copy(s + AHEAD, 0).start()
 
-        @pl.when(s >= 2)
-        def _():
-            t = s - 2
-            hop_arrival(t, 2).wait_recv()
-            sib_copy(t, 3).start()
+        @pl.when((s >= 2) & (s < STEPS + 2))
+        def _():
+            hop_arrival(s - 2, 2).wait_recv()
+            sib_copy(s - 2, 3).start()
+
+        @pl.when(s >= 3)
+        def _():
+            t = s - 3
             for n in range(4):
                 sib_arrival(t, n).wait_recv()
             weight_part(t)
 
-        @pl.when(s > 9)
-        def _():
-            @pl.loop(jnp.where(s == STEPS + 1, 15, 2 * s - 20), jnp.where(s == STEPS, 15, 2 * s - 18))
+        @pl.when(s >= 8)
+        def _():
+            catch_up = s <= 12
+
+            @pl.loop(jnp.where(catch_up, 2 * s - 16, s - 3), jnp.where(catch_up, 2 * s - 14, s - 2))
             def _(r):
                 head_part(r)
 
@@ -325,7 +329,7 @@
                 w_copy(0, m).wait_send()
                 w_copy(1, m).wait_send()
 
-        @pl.when(s == 14)
+        @pl.when(s == 13)
         def _():
             collect(0, 0, 16)
 
@@ -336,7 +340,7 @@
 
             pair_copy().start()
 
-        @pl.when(s == STEPS)
+        @pl.when(s == STEPS + 1)
         def _():
             collect(1, 0, 12)
 

time: 156 us -> 151 us (0.968)
  the two profiles are of different devices: /device:TPU:29 before, /device:TPU:24 now
where the time goes in v3:
time: 151 us
  Pallas kernels  150 us (99%)
    pallas_call x1, Pallas kernels, on_device(): pl.pallas_call(kernel, out_shape=(jax.ShapeDtypeStruct((ROWS, COLS), BF),...  147 us

profile of v3, /device:TPU:24, one launch (start us, length us, event | category | flops | bytes accessed | tf_op | source)
XLA Modules:
  0.0 150.8 jit_solution(6267309158469608747)
XLA Ops:
  0.6 147.4 %attention_backward.1 = (bf16[1024,384]{1,0:T(8,128)(2,1)}, bf16[1024,384]{1,0:T(8,128)(2,1)}, bf16[1024,384]{1,0:T(8,128)(2,1)}, f32[192,384]{1,0:T(8,128)}) custom-call(bf16[128,6144]{1,0:T(8,128)(2,1)} %grad_hbm.1, bf16[1024,384]{1,0:T(8,128)(2,1)} %q_hbm.1, bf16[1024,384]{1,0:T(8,128)(2,1)} %k_hbm.1, bf16[1024,384]{1,0:T(8,128)(2,1)} %v_hbm.1, ...), custom_call_target="tpu_custom_call" | custom-call | flops 12999999488 | bytes 30000000 | tf_op jit(solution)/shard_map/attention_backward/pallas_call | solution.py:404
  148.1 2.7 %place_outputs.1 = (bf16[1024,384]{1,0:T(8,128)(2,1)}, bf16[1024,384]{1,0:T(8,128)(2,1)}, bf16[1024,384]{1,0:T(8,128)(2,1)}, f32[192,384]{1,0:T(8,128)}) custom-call(bf16[1024,384]{1,0:T(8,128)(2,1)} %get-tuple-element.12.refs_0_, bf16[1024,384]{1,0:T(8,128)(2,1)} %get-tuple-element.13.refs_1_, bf16[1024,384]{1,0:T(8,128)(2,1)} %get-tuple-element.14.refs_2_, ...), custom_call_target="tpu_custom_call" | custom-call | tf_op jit(solution)/shard_map/place_outputs/pallas_call | solution.py:444

commit v4 on v3

--- a/solution.py
+++ b/solution.py
@@ -340,7 +340,7 @@
 
             pair_copy().start()
 
-        @pl.when(s == STEPS + 1)
+        @pl.when(s == STEPS + 2)
         def _():
             collect(1, 0, 12)
 

time: 151 us -> 149 us (0.987)
    pallas_call x1, Pallas kernels: 147 us -> 146 us  [on_device(): pl.pallas_call(kernel, out_shape=(jax.ShapeDtypeStruct((ROWS, COLS), BF),...]
where the time goes in v4:
time: 149 us
  Pallas kernels  149 us (100%)
    pallas_call x1, Pallas kernels, on_device(): pl.pallas_call(kernel, out_shape=(jax.ShapeDtypeStruct((ROWS, COLS), BF),...  146 us

profile of v4, /device:TPU:24, one launch (start us, length us, event | category | flops | bytes accessed | tf_op | source)
XLA Modules:
  0.0 149.2 jit_solution(5223868918687191119)
XLA Ops:
  0.6 145.9 %attention_backward.1 = (bf16[1024,384]{1,0:T(8,128)(2,1)}, bf16[1024,384]{1,0:T(8,128)(2,1)}, bf16[1024,384]{1,0:T(8,128)(2,1)}, f32[192,384]{1,0:T(8,128)}) custom-call(bf16[128,6144]{1,0:T(8,128)(2,1)} %grad_hbm.1, bf16[1024,384]{1,0:T(8,128)(2,1)} %q_hbm.1, bf16[1024,384]{1,0:T(8,128)(2,1)} %k_hbm.1, bf16[1024,384]{1,0:T(8,128)(2,1)} %v_hbm.1, ...), custom_call_target="tpu_custom_call" | custom-call | flops 12999999488 | bytes 30000000 | tf_op jit(solution)/shard_map/attention_backward/pallas_call | solution.py:404
  146.5 2.7 %place_outputs.1 = (bf16[1024,384]{1,0:T(8,128)(2,1)}, bf16[1024,384]{1,0:T(8,128)(2,1)}, bf16[1024,384]{1,0:T(8,128)(2,1)}, f32[192,384]{1,0:T(8,128)}) custom-call(bf16[1024,384]{1,0:T(8,128)(2,1)} %get-tuple-element.12.refs_0_, bf16[1024,384]{1,0:T(8,128)(2,1)} %get-tuple-element.13.refs_1_, bf16[1024,384]{1,0:T(8,128)(2,1)} %get-tuple-element.14.refs_2_, ...), custom_call_target="tpu_custom_call" | custom-call | tf_op jit(solution)/shard_map/place_outputs/pallas_call | solution.py:444
